TPU v7x, 32 devices: a whole 2x2x4 slice. The times are simulated.
32 devices in a mesh: group: 2 (over x), fsdp: 8 (over z, y), tp: 2 (over core).
Axes of the slice: x: 2, y: 2, z: 4, core: 2. Of those that a mesh axis runs over, the one named last changes fastest.
Arguments:
- inputs: bfloat16 [8192, 8192], P(('group', 'fsdp'), 'tp'), parts along dimension 0, may hold values from -6 to 6
- value_gradient: bfloat16 [8192, 1024], P(('group', 'fsdp'), 'tp'), parts along dimension 0, may hold values from -6 to 6
- fixed_projection_matrix: bfloat16 [8192, 1024], P('fsdp', 'tp'), may hold values from -0.0625 to 0.0625
- adapter_down_weight: bfloat16 [16, 16, 8192], P(('group', 'fsdp'), None, 'tp'), parts along dimension 0, may hold values from -0.0625 to 0.0625
- adapter_up_weight: bfloat16 [16, 16, 1024], P(('group', 'fsdp'), None, 'tp'), parts along dimension 0, may hold values from -0.1875 to 0.1875
- live_token_count: int32 [16], P('group'), parts along dimension 0, may hold values from 1 to 2048, as said below
- adapter_storage_row: int32 [16], P('group'), parts along dimension 0, may hold values from 0 to 7, each once
Outputs:
- input_gradient: bfloat16 [8192, 8192], P(('group', 'fsdp'), 'tp'), parts along dimension 0
- lowering_sensitivity: float32 [16, 16, 8192], P(('group', 'fsdp'), None, 'tp'), parts along dimension 0
- raising_sensitivity: float32 [16, 16, 1024], P(('group', 'fsdp'), None, 'tp'), parts along dimension 0
There are 2 independent parts, one for each index of `group`. A program takes and returns all parts, laid end to end along the dimension named above; an argument that names none is the same for every part. Nothing has to cross between parts.
Inputs may be any that keep to these rules, and one draw needn't show every extreme that they name: `live_token_count`: the padded block counts ceil(c / 128) sum to 32; exactly one adapter has 16 blocks and 2048 live tokens, every adapter has at least one live token. `adapter_storage_row`: each storage row holds exactly one adapter.
All inputs are finite; a program needn't handle non-finite values.
Results may differ from a plain program's by a relative error of at most 0.0031.
Values may be sent and summed in bfloat16 or wider, within the bound.
A program may use at most 128 MiB of HBM per device.

v0:
```python
import jax
import jax.numpy as jnp
from jax import lax
from jax.sharding import PartitionSpec as P

BLOCK = 128


adapter_scale = 2.0


def shards(
    inputs,
    value_gradient,
    fixed_projection_matrix,
    adapter_down_weight,
    adapter_up_weight,
    live_token_count,
    adapter_storage_row,
):
    token_rows = inputs.shape[0]
    half_width = inputs.shape[1]
    heads_half = value_gradient.shape[1]
    adapter_total = live_token_count.shape[0]
    block_count = token_rows // BLOCK
    place_offset = lax.axis_index("fsdp")
    blocks_of = (live_token_count + BLOCK - 1) // BLOCK
    stop_marks = jnp.cumsum(blocks_of)
    firsts = stop_marks - blocks_of
    segment_labels = place_offset * block_count + jnp.arange(block_count, dtype=jnp.int32)
    owner_adapter = jnp.sum(
        (stop_marks[None, :] <= segment_labels[:, None]).astype(jnp.int32), axis=1
    )
    owner_hot = jnp.arange(adapter_total, dtype=jnp.int32)[None, :] == owner_adapter[:, None]
    count_block = jnp.sum(jnp.where(owner_hot, live_token_count[None, :], 0), axis=1)
    first_block = jnp.sum(jnp.where(owner_hot, firsts[None, :], 0), axis=1)
    position_segment = jnp.sum(jnp.where(owner_hot, adapter_storage_row[None, :], 0), axis=1)
    offsets = jnp.arange(BLOCK, dtype=jnp.int32)
    live = (segment_labels[:, None] - first_block[:, None]) * BLOCK + offsets[
        None, :
    ] < count_block[:, None]
    grad_blocks = value_gradient.reshape(block_count, BLOCK, heads_half)
    masked_tokens = jnp.where(live[:, :, None], grad_blocks, jnp.zeros_like(grad_blocks))
    source_segments = inputs.reshape(block_count, BLOCK, half_width)
    every_lowering_factor, up_all = (
        lax.all_gather(adapter_down_weight, "fsdp", axis=0, tiled=True),
        lax.all_gather(adapter_up_weight, "fsdp", axis=0, tiled=True),
    )
    picked_lowering_factor = jnp.take(every_lowering_factor, position_segment, axis=0)
    up_sel = jnp.take(up_all, position_segment, axis=0)
    low_part = jnp.einsum(
        "nsm,nxm->nsx", source_segments, picked_lowering_factor, preferred_element_type=jnp.float32
    )
    inner_grad_piece = jnp.einsum(
        "btk,brk->btr", masked_tokens, up_sel, preferred_element_type=jnp.float32
    )
    low_sum, middle_gradient_sum = lax.psum((low_part, inner_grad_piece), "tp")
    reduced_activation = low_sum.astype(jnp.bfloat16)
    narrow_backflow = (adapter_scale * middle_gradient_sum).astype(jnp.bfloat16)
    adapter_contribution = jnp.einsum(
        "njc,ncd->njd", narrow_backflow, picked_lowering_factor, preferred_element_type=jnp.float32
    )
    down_terms = jnp.einsum(
        "btr,bth->brh", narrow_backflow, source_segments, preferred_element_type=jnp.float32
    )
    up_contributions = adapter_scale * jnp.einsum(
        "btr,btk->brk", reduced_activation, masked_tokens, preferred_element_type=jnp.float32
    )
    slot_hot = (
        jnp.arange(adapter_total, dtype=jnp.int32)[None, :] == position_segment[:, None]
    ).astype(jnp.float32)
    dense_down = jnp.einsum("ba,brh->arh", slot_hot, down_terms, precision=lax.Precision.HIGHEST)
    dense_up = jnp.einsum(
        "ba,brk->ark", slot_hot, up_contributions, precision=lax.Precision.HIGHEST
    )
    sent_down = dense_down[:, None, :, :]
    sent_up = dense_up[:, None, :, :]
    recv_down, recv_up = (
        lax.all_to_all(sent_down, "fsdp", split_axis=0, concat_axis=1, tiled=True),
        lax.all_to_all(sent_up, "fsdp", split_axis=0, concat_axis=1, tiled=True),
    )
    lowering_sensitivity = jnp.sum(recv_down, axis=1)
    raising_sensitivity = jnp.sum(recv_up, axis=1)
    masked_rows = masked_tokens.reshape(token_rows, heads_half)
    every_feature = lax.dot_general(
        masked_rows,
        lax.all_gather(fixed_projection_matrix, "fsdp", axis=0, tiled=True),
        (((1,), (1,)), ((), ())),
        preferred_element_type=jnp.float32,
    )
    frozen_output = lax.psum_scatter(every_feature, "tp", scatter_dimension=1, tiled=True)
    input_gradient = (frozen_output + adapter_contribution.reshape(token_rows, half_width)).astype(
        jnp.bfloat16
    )
    return (input_gradient, lowering_sensitivity, raising_sensitivity)


def solution(mesh):
    in_specs = (
        P(("group", "fsdp"), "tp"),
        P(("group", "fsdp"), "tp"),
        P("fsdp", "tp"),
        P(("group", "fsdp"), None, "tp"),
        P(("group", "fsdp"), None, "tp"),
        P("group"),
        P("group"),
    )
    out_specs = (
        P(("group", "fsdp"), "tp"),
        P(("group", "fsdp"), None, "tp"),
        P(("group", "fsdp"), None, "tp"),
    )
    return jax.shard_map(shards, mesh=mesh, in_specs=in_specs, out_specs=out_specs, check_vma=False)
```

profile of v0, /device:TPU:1, one launch (start us, length us, event | category | flops | bytes accessed | tf_op | source)
XLA Modules:
  0.0 276.1 jit_solution(6284585652604469807)
XLA Ops:
  7.2 0.0 all-gather.3.cloned.1.call-start
  7.2 0.7 all-gather.3.cloned.1.call-update
  7.9 0.0 all-gather.5.cloned.1.call-start
  7.9 0.7 all-gather.5.cloned.1.call-update
  8.6 0.0 reduce-scatter.2.cloned.1.call-start
  8.7 0.7 fusion.35
  9.4 0.2 reduce-window.8
  9.6 0.7 bitcast_subtract_fusion
  10.2 0.2 convert_reduce_fusion
  10.4 0.9 select_reduce_fusion
  11.3 0.1 fusion.34
  11.4 125.4 %all-gather.3.cloned.1.call-done = bf16[8192,512]{1,0:T(8,128)(2,1)} async-done(((bf16[1024,512]{1,0:T(8,128)(2,1)}), bf16[8192,512]{1,0:T(8,128)(2,1)}) %all-gather.3.cloned.1.call-update) | async-done | bytes 8388624 | tf_op jit(solution)/shard_map/all_gather | solution.py:87
  136.8 13.9 %fusion.2 = f32[512,8192]{1,0:T(8,128)} fusion(bf16[8192,512]{1,0:T(8,128)(2,1)} %all-gather.3.cloned.1.call-done, bf16[512,512]{1,0:T(8,128)(2,1)} %param.8, pred[512]{0:T(512)(128)(4,1)S(1)} %fusion.34), kind=kOutput, calls=%fused_computation.9 | convolution fusion | flops 4295229440 | bytes 25690624 | tf_op jit(solution)/shard_map/dot_general | solution.py:85
  150.6 0.0 copy-start.1
  150.6 0.0 copy-start
  150.6 0.0 reduce-scatter.2.cloned.1.call-update
  150.7 0.7 copy-done.1
  151.3 24.8 %all_gather.10 = bf16[8,16,512]{2,1,0:T(8,128)(2,1)S(1)} all-gather(bf16[1,16,512]{2,1,0:T(8,128)(2,1)S(1)} %copy-done.1), channel_id=1, replica_groups=mesh['group'=2,'fsdp'=8,'tp'=2] {'fsdp'}, dimensions={0}, use_global_device_ids=true | all-gather | bytes 147456 | tf_op jit(solution)/shard_map/all_gather | solution.py:47
  176.2 0.6 gather_fusion
  176.8 0.1 add_compare_fusion
  176.8 0.0 copy-done
  176.8 0.3 fusion.5
  177.2 0.0 all-gather.5.cloned.1.call-done
  177.2 1.8 gather_fusion.1
  179.0 3.4 %convolution_bitcast_fusion.2 = f32[4,128,16]{1,2,0:T(8,128)S(1)} fusion(bf16[4,128,4096]{2,1,0:T(8,128)(2,1)} %bitcast.32, bf16[4,16,4096]{2,1,0:T(8,128)(2,1)S(1)} %gather_fusion.1, pred[4]{0:T(512)(128)(4,1)S(1)} %compare_and_fusion), kind=kOutput, calls=%fused_computation.7 | convolution fusion | flops 67371008 | bytes 4751364 | tf_op jit(solution)/shard_map/nsm,nxm->nsx/dot_general | solution.py:51
  182.4 10.8 %all-reduce = (f32[4,128,16]{1,2,0:T(8,128)S(1)}, bf16[4,128,16]{1,2,0:T(8,128)(2,1)S(1)}) all-reduce(f32[4,128,16]{1,2,0:T(8,128)S(1)} %fusion.5, f32[4,128,16]{1,2,0:T(8,128)S(1)} %convolution_bitcast_fusion.2), channel_id=1, replica_groups=mesh['group'=2,'fsdp'=8,'tp'=2] {'tp'}, use_global_device_ids=true, to_apply=%region_6.7 | all-reduce | flops 16384 | bytes 114688 | tf_op jit(solution)/shard_map/psum | solution.py:57
  193.2 0.3 convolution_multiply_fusion
  193.5 0.4 convolution_bitcast_fusion.1
  193.9 0.9 copy.15
  194.7 3.4 %all-to-all-start.1 = ((f32[8,1,16,512]{3,2,1,0:T(8,128)}), f32[8,1,16,512]{3,2,1,0:T(8,128)S(1)}, u32[]{:S(2)}, u32[]{:S(2)}) async-start(f32[8,1,16,512]{3,2,1,0:T(8,128)} %copy.15), calls=%async_computation.2 | async-start | bytes 524288 | tf_op jit(solution)/shard_map/all_to_all | solution.py:80
  198.2 3.8 %fusion.15 = f32[4,16,4096]{2,1,0:T(8,128)S(1)} fusion(bf16[4,128,4096]{2,1,0:T(8,128)(2,1)} %bitcast.33, f32[4,128,16]{1,2,0:T(8,128)S(1)} %get-tuple-element.6), kind=kOutput, calls=%fused_computation.25 | convolution fusion | flops 67125248 | bytes 5275648 | tf_op jit(solution)/shard_map/btr,bth->brh/dot_general | solution.py:63
  201.9 1.9 convolution_bitcast_fusion
  203.9 2.5 copy.13
  206.4 0.7 all-to-all-done.1
  207.1 4.9 %all-to-all-start = ((f32[8,1,16,4096]{3,2,1,0:T(8,128)}), f32[8,1,16,4096]{3,2,1,0:T(8,128)S(1)}, u32[]{:S(2)}, u32[]{:S(2)}) async-start(f32[8,1,16,4096]{3,2,1,0:T(8,128)} %copy.13), calls=%async_computation.1 | async-start | bytes 4194304 | tf_op jit(solution)/shard_map/all_to_all | solution.py:79
  211.9 4.5 %fusion.9 = f32[4,128,4096]{2,1,0:T(8,128)} fusion(bf16[4,16,4096]{2,1,0:T(8,128)(2,1)S(1)} %gather_fusion.1, pred[4]{0:T(512)(128)(4,1)S(1)} %compare_and_fusion, f32[4,128,16]{1,2,0:T(8,128)S(1)} %get-tuple-element.6), kind=kOutput, calls=%fused_computation.18 | convolution fusion | flops 67387392 | bytes 8945668 | tf_op jit(solution)/shard_map/njc,ncd->njd/dot_general | solution.py:60
  216.5 0.6 reduce_sum.67
  217.1 42.6 %all-to-all-done = f32[8,1,16,4096]{3,2,1,0:T(8,128)S(1)} async-done(((f32[8,1,16,4096]{3,2,1,0:T(8,128)}), f32[8,1,16,4096]{3,2,1,0:T(8,128)S(1)}, u32[]{:S(2)}, u32[]{:S(2)}) %all-to-all-start) | async-done | bytes 2097184 | tf_op jit(solution)/shard_map/all_to_all | solution.py:79
  259.7 0.8 reduce_sum.65
  260.5 0.0 reduce-scatter.2.cloned.1.call-done
  260.5 9.0 %fusion = bf16[512,4096]{1,0:T(8,128)(2,1)} fusion(f32[512,4096]{1,0:T(8,128)} %reduce-scatter.2.cloned.1.call-done, f32[4,128,4096]{2,1,0:T(8,128)} %fusion.9), kind=kLoop, calls=%fused_computation.3 | loop fusion | flops 4194304 | bytes 20971520 | tf_op jit(solution)/shard_map/convert_element_type | solution.py:92
  (5 shorter events, 0.0 us)
Async XLA Ops:
  7.2 129.6 %all-gather.3.cloned.1.call-start = ((), (), s32[]{:S(2)}) async-start(), calls=%async_computation.3 | async-start | bytes 9437184 | tf_op jit(solution)/shard_map/all_gather | solution.py:87
  7.9 169.3 %all-gather.5.cloned.1.call-start = ((), (), s32[]{:S(2)}) async-start(), calls=%async_computation.5 | async-start | bytes 1179648 | tf_op jit(solution)/shard_map/all_gather | solution.py:46
  8.6 251.9 %reduce-scatter.2.cloned.1.call-start = ((), (), s32[]{:S(2)}) async-start(), calls=%async_computation.4 | async-start | bytes 25165824 | tf_op jit(solution)/shard_map/reduce_scatter | solution.py:91
  150.6 0.7 copy-start.1
  150.6 26.2 %copy-start = (bf16[512,512]{1,0:T(8,128)(2,1)S(1)}, bf16[512,512]{1,0:T(8,128)(2,1)}, u32[]{:S(2)}) copy-start(bf16[512,512]{1,0:T(8,128)(2,1)} %param.8) | copy-start | bytes 1572868
  194.7 12.3 %all-to-all-start.1 = ((f32[8,1,16,512]{3,2,1,0:T(8,128)}), f32[8,1,16,512]{3,2,1,0:T(8,128)S(1)}, u32[]{:S(2)}, u32[]{:S(2)}) async-start(f32[8,1,16,512]{3,2,1,0:T(8,128)} %copy.15), calls=%async_computation.2 | async-start | bytes 524288 | tf_op jit(solution)/shard_map/all_to_all | solution.py:80
  207.1 52.7 %all-to-all-start = ((f32[8,1,16,4096]{3,2,1,0:T(8,128)}), f32[8,1,16,4096]{3,2,1,0:T(8,128)S(1)}, u32[]{:S(2)}, u32[]{:S(2)}) async-start(f32[8,1,16,4096]{3,2,1,0:T(8,128)} %copy.13), calls=%async_computation.1 | async-start | bytes 4194304 | tf_op jit(solution)/shard_map/all_to_all | solution.py:79
Sparse Core Ops, SparseCore 0:
  10.1 126.5 all-gather.2
  138.9 38.1 all-gather.4
  179.4 26.5 reduce-scatter.1
where the time goes:
time: 278 us; the launch traced here: 276 us
  waiting for transfers between devices  170 us (61%)
  blocking collectives  35.6 us (13%)
  matrix products  28.5 us (10%)
  between operations  13.8 us (5%)
  other arithmetic  13.2 us (5%)
  starting transfers between devices  8.42 us (3%)
  local copies, waits for them, and re-layouts  6.46 us (2%)
    all_gather x1, waiting for transfers between devices, shards(): lax.all_gather(fixed_projection_matrix, 'fsdp', axis=0, tiled=True)  125 us
    all_to_all x1, waiting for transfers between devices, shards(): lax.all_to_all(sent_down, 'fsdp', split_axis=0, concat_axis=1, tiled=True)  42.6 us
    all_gather x1, blocking collectives, shards(): lax.all_gather(adapter_up_weight, 'fsdp', axis=0, tiled=True)  24.8 us
    dot_general x1, matrix products, shards(): lax.dot_general(masked_rows, lax.all_gather(fixed_projection_matrix, 'fsd...  13.9 us
    psum x1, blocking collectives, shards(): low_sum, middle_gradient_sum = lax.psum((low_part, inner_grad_piece), 'tp')  10.8 us
    convert_element_type x1, other arithmetic, shards(): (frozen_output + adapter_contribution.reshape(token_rows, half_width)).as...  9.01 us
  transfers between devices with their start and end apart: 5, of which 3 were waited for; matrix products, arithmetic and copies ran while one was open for 14% of the time, Pallas kernels for 0%

commit v1 on v0

--- a/solution.py
+++ b/solution.py
@@ -1,6 +1,10 @@
+import functools
+
 import jax
 import jax.numpy as jnp
 from jax import lax
+from jax.experimental import pallas as pl
+from jax.experimental.pallas import tpu as pltpu
 from jax.sharding import PartitionSpec as P
 
 BLOCK = 128
@@ -95,6 +99,359 @@
     return (input_gradient, lowering_sensitivity, raising_sensitivity)
 
 
+F32 = jnp.float32
+BF16 = jnp.bfloat16
+
+
+def nt(a, b):
+    return lax.dot_general(a, b, (((1,), (1,)), ((), ())), preferred_element_type=F32)
+
+
+def fused_kernel(
+    fsdp_total,
+    x_ref, dv_ref, w_ref, a_ref, b_ref, cnt_ref, row_ref,
+    ig_ref, lo_ref, ra_ref,
+    wall, dvb, a_all, b_all, mask, gm, gm_t, psend, precv,
+    lsend, lrecv, lfull, rsend, rrecv, osend, orecv,
+    ch_s, ch_r, y_s, y_r, sb_s, sb_r, a_s, a_r, b_s, b_r,
+    l_s, l_r, r_s, r_r, dv_s, dv_r, p_s, p_r, o_s, o_r,
+):
+    depth = fsdp_total // 2
+    half = depth // 2
+    tokens, width = x_ref.shape
+    heads = dv_ref.shape[1]
+    rank = a_ref.shape[1]
+    slots = fsdp_total * rank
+    rows = w_ref.shape[0] // 2
+    g = lax.axis_index("group")
+    f = lax.axis_index("fsdp")
+    c = lax.axis_index("tp")
+    z = f // 2
+    y = f % 2
+    lo = c * half
+    sibling = (g, f, 1 - c)
+    twin = (1 - g, f, c)
+
+    def remote(src, dst, ss, rs, dev):
+        return pltpu.make_async_remote_copy(
+            src_ref=src, dst_ref=dst, send_sem=ss, recv_sem=rs,
+            device_id=dev, device_id_type=pl.DeviceIdType.MESH,
+        )
+
+    barrier = pltpu.get_barrier_semaphore()
+    for k in range(1, fsdp_total):
+        pl.semaphore_signal(
+            barrier, inc=1, device_id=(g, lax.rem(f + k, fsdp_total), c),
+            device_id_type=pl.DeviceIdType.MESH,
+        )
+    for dev in (sibling, twin, (g, z * 2 + 1 - y, 1 - c)):
+        pl.semaphore_signal(barrier, inc=1, device_id=dev, device_id_type=pl.DeviceIdType.MESH)
+
+    wall[z, y, c] = w_ref[pl.ds(pl.multiple_of(g * rows, rows), rows), :]
+    mine = pl.ds(pl.multiple_of(f * rank, rank), rank)
+    a_all[mine, :] = a_ref[0]
+    b_all[mine, :] = b_ref[0]
+    token = f * tokens + lax.broadcasted_iota(jnp.int32, (tokens, slots), 0)
+    lane_row = lax.broadcasted_iota(jnp.int32, (tokens, slots), 1) // rank
+    start = jnp.int32(0)
+    alive = jnp.zeros((tokens, slots), F32)
+    any_live = jnp.zeros((tokens, slots), F32)
+    for a in range(fsdp_total):
+        count = cnt_ref[a]
+        blocks = (count + (BLOCK - 1)) // BLOCK
+        inside = jnp.where((token >= start) & (token < start + count), 1.0, 0.0)
+        any_live = any_live + inside
+        alive = alive + jnp.where(lane_row == row_ref[a], inside, 0.0)
+        start = start + blocks * BLOCK
+    mask[...] = alive
+    live_column = any_live[:, :1]
+    dvb[0, c] = jnp.where(live_column > 0.5, dv_ref[...].astype(F32), 0.0).astype(BF16)
+
+    pl.semaphore_wait(barrier, fsdp_total + 2)
+
+    def dv_copy(i):
+        if i == 0:
+            return remote(dvb.at[0, c], dvb.at[0, c], dv_s.at[0], dv_r.at[0], sibling)
+        if i == 1:
+            return remote(dvb.at[0, c], dvb.at[1, c], dv_s.at[1], dv_r.at[1], twin)
+        return remote(dvb.at[1, c], dvb.at[1, c], dv_s.at[2], dv_r.at[2], sibling)
+
+    def piece(zp):
+        return wall.at[zp, y, c]
+
+    def chain_copy(zp, up):
+        to = z + 1 if up else z - 1
+        return remote(piece(zp), piece(zp), ch_s.at[zp, 1 if up else 0], ch_r.at[zp], (g, to * 2 + y, c))
+
+    def y_copy(zp):
+        core = zp // half
+        return remote(piece(zp), piece(zp), y_s.at[zp], y_r.at[zp, c], (g, z * 2 + 1 - y, core))
+
+    def sib_copy(zp):
+        return remote(piece(zp), piece(zp), sb_s.at[zp], sb_r.at[zp], sibling)
+
+    def b_copy(j):
+        return remote(b_all.at[mine, :], b_all.at[mine, :], b_s.at[j], b_r.at[f], (g, j, c))
+
+    def a_copy(j):
+        return remote(a_all.at[mine, :], a_all.at[mine, :], a_s.at[j], a_r.at[f], (g, j, c))
+
+    def peers(fn):
+        def step(k, carry):
+            fn(lax.rem(f + k, fsdp_total))
+            return carry
+        lax.fori_loop(1, fsdp_total, step, 0)
+
+    def rank_rows(j):
+        return pl.ds(pl.multiple_of(j * rank, rank), rank)
+
+    def wait_in(dst, sem):
+        remote(dst, dst, sem, sem, sibling).wait_recv()
+
+    def spread(zp):
+        y_copy(zp).start()
+
+        @pl.when(zp // half != c)
+        def _():
+            sib_copy(zp).start()
+
+    dv_copy(0).start()
+    peers(lambda j: b_copy(j).start())
+
+    @pl.when(z < depth - 1)
+    def _():
+        chain_copy(z, True).start()
+
+    @pl.when(z > 0)
+    def _():
+        chain_copy(z, False).start()
+
+    dv_copy(1).start()
+    spread(z)
+    peers(lambda j: a_copy(j).start())
+
+    peers(lambda j: wait_in(b_all.at[rank_rows(j), :], b_r.at[j]))
+    psend[0] = nt(dvb[0, c], b_all[...])
+    gm_copy = remote(psend.at[0], precv.at[0], p_s.at[0], p_r.at[0], sibling)
+    gm_copy.start()
+    gm_copy.wait_recv()
+    total = adapter_scale * (psend[0] + precv[0])
+    total = jnp.where(mask[...] > 0.5, total, 0.0)
+    gm[...] = total.astype(BF16)
+    gm_t[...] = total.T.astype(BF16)
+
+    chunk = 512
+
+    def lower(i, carry):
+        cols = pl.ds(pl.multiple_of(i * chunk, chunk), chunk)
+        term = jnp.dot(gm_t[...], x_ref[:, cols], preferred_element_type=F32)
+        lfull[:, cols] = term
+        lsend[:, cols] = term.astype(BF16)
+        return carry
+
+    lax.fori_loop(0, width // chunk, lower, 0)
+
+    def l_copy(j):
+        return remote(lsend.at[rank_rows(j), :], lrecv.at[mine, :], l_s.at[j], l_r.at[f], (g, j, c))
+
+    peers(lambda j: l_copy(j).start())
+
+    wait_in(dvb.at[1, c], dv_r.at[1])
+    dv_copy(2).start()
+
+    peers(lambda j: wait_in(a_all.at[rank_rows(j), :], a_r.at[j]))
+    psend[1] = jnp.zeros((tokens, slots), F32)
+
+    def low_step(i, carry):
+        cols = pl.ds(pl.multiple_of(i * chunk, chunk), chunk)
+        psend[1] = psend[1] + nt(x_ref[:, cols], a_all[:, cols])
+        return carry
+
+    lax.fori_loop(0, width // chunk, low_step, 0)
+    low_copy = remote(psend.at[1], precv.at[1], p_s.at[1], p_r.at[1], sibling)
+    low_copy.start()
+    low_copy.wait_recv()
+    low = jnp.where(mask[...] > 0.5, psend[1] + precv[1], 0.0)
+    up_term = adapter_scale * jnp.dot(low.T.astype(BF16), dvb[0, c], preferred_element_type=F32)
+    rsend[...] = up_term
+
+    def r_copy(j):
+        return remote(rsend.at[rank_rows(j), :], rrecv.at[mine, :], r_s.at[j], r_r.at[f], (g, j, c))
+
+    peers(lambda j: r_copy(j).start())
+    wait_in(dvb.at[0, 1 - c], dv_r.at[0])
+    wait_in(dvb.at[1, 1 - c], dv_r.at[2])
+
+    def o_copy(tile):
+        return remote(osend.at[tile], orecv.at[tile], o_s.at[tile], o_r.at[tile], twin)
+
+    def columns(tile, which):
+        return pl.ds(pl.multiple_of(tile * (2 * rows) + which * rows, rows), rows)
+
+    def tiles(zt):
+        wait_in(wall.at[zt, y, 1 - c], sb_r.at[zt])
+        for other in (0, 1):
+            yp = 1 - y if other else y
+            if other:
+                wait_in(wall.at[zt, yp, 0], y_r.at[zt, 0])
+                wait_in(wall.at[zt, yp, 1], y_r.at[zt, 1])
+            tile = (zt - lo) * 2 + yp
+            osend[tile] = (nt(dvb[1, 0], wall[zt, yp, 0]) + nt(dvb[1, 1], wall[zt, yp, 1])).astype(BF16)
+            o_copy(tile).start()
+            cols = columns(tile, g)
+            ig_ref[:, cols] = (
+                nt(dvb[0, 0], wall[zt, yp, 0])
+                + nt(dvb[0, 1], wall[zt, yp, 1])
+                + jnp.dot(gm[...], a_all[:, cols], preferred_element_type=F32)
+            ).astype(BF16)
+
+    def in_half(zp):
+        return (zp >= lo) & (zp < lo + half)
+
+    def step(d, carry):
+        @pl.when(z - d >= 0)
+        def _():
+            wait_in(piece(z - d), ch_r.at[z - d])
+
+            @pl.when(z < depth - 1)
+            def _():
+                chain_copy(z - d, True).start()
+
+            spread(z - d)
+
+        @pl.when(z + d < depth)
+        def _():
+            wait_in(piece(z + d), ch_r.at[z + d])
+
+            @pl.when(z > 0)
+            def _():
+                chain_copy(z + d, False).start()
+
+            spread(z + d)
+
+        zt = jnp.where(in_half(z + d - 1), z + d - 1, z - d + 1)
+
+        @pl.when(in_half(zt))
+        def _():
+            tiles(zt)
+
+        return carry
+
+    lax.fori_loop(1, depth + 1, step, 0)
+
+    def finish(tile, carry):
+        wait_in(orecv.at[tile], o_r.at[tile])
+        cols = columns(tile, 1 - g)
+        ig_ref[:, cols] = (
+            orecv[tile].astype(F32)
+            + jnp.dot(gm[...], a_all[:, cols], preferred_element_type=F32)
+        ).astype(BF16)
+        return carry
+
+    lax.fori_loop(0, 2 * half, finish, 0)
+
+    lo_ref[0] = lfull[mine, :]
+    ra_ref[0] = rsend[mine, :]
+
+    def add_terms(j):
+        wait_in(lrecv.at[rank_rows(j), :], l_r.at[j])
+        lo_ref[0] = lo_ref[0] + lrecv[rank_rows(j), :].astype(F32)
+        wait_in(rrecv.at[rank_rows(j), :], r_r.at[j])
+        ra_ref[0] = ra_ref[0] + rrecv[rank_rows(j), :]
+
+    peers(add_terms)
+
+    for i in range(3):
+        dv_copy(i).wait_send()
+    gm_copy.wait_send()
+    low_copy.wait_send()
+
+    def sent(j):
+        a_copy(j).wait_send()
+        b_copy(j).wait_send()
+        l_copy(j).wait_send()
+        r_copy(j).wait_send()
+
+    peers(sent)
+
+    def sent_tile(tile, carry):
+        o_copy(tile).wait_send()
+        return carry
+
+    lax.fori_loop(0, 2 * half, sent_tile, 0)
+
+    def sent_piece(zp, carry):
+        @pl.when((zp <= z) & (z < depth - 1))
+        def _():
+            chain_copy(zp, True).wait_send()
+
+        @pl.when((zp >= z) & (z > 0))
+        def _():
+            chain_copy(zp, False).wait_send()
+
+        y_copy(zp).wait_send()
+
+        @pl.when(zp // half != c)
+        def _():
+            sib_copy(zp).wait_send()
+
+        return carry
+
+    lax.fori_loop(0, depth, sent_piece, 0)
+
+
+def fused(fsdp_total, x, dv, w, a, b, counts, storage):
+    tokens, width = x.shape
+    heads = dv.shape[1]
+    rank = a.shape[1]
+    slots = fsdp_total * rank
+    depth = fsdp_total // 2
+    half = depth // 2
+    rows = w.shape[0] // 2
+    vmem = pl.BlockSpec(memory_space=pltpu.VMEM)
+    smem = pl.BlockSpec(memory_space=pltpu.SMEM)
+    dma = pltpu.SemaphoreType.DMA
+    n = fsdp_total
+    return pl.pallas_call(
+        functools.partial(fused_kernel, fsdp_total),
+        out_shape=(
+            jax.ShapeDtypeStruct((tokens, width), BF16),
+            jax.ShapeDtypeStruct((1, rank, width), F32),
+            jax.ShapeDtypeStruct((1, rank, heads), F32),
+        ),
+        in_specs=[vmem] * 5 + [smem] * 2,
+        out_specs=(vmem,) * 3,
+        scratch_shapes=[
+            pltpu.VMEM((depth, 2, 2, rows, heads), BF16),
+            pltpu.VMEM((2, 2, tokens, heads), BF16),
+            pltpu.VMEM((slots, width), BF16),
+            pltpu.VMEM((slots, heads), BF16),
+            pltpu.VMEM((tokens, slots), F32),
+            pltpu.VMEM((tokens, slots), BF16),
+            pltpu.VMEM((slots, tokens), BF16),
+            pltpu.VMEM((2, tokens, slots), F32),
+            pltpu.VMEM((2, tokens, slots), F32),
+            pltpu.VMEM((slots, width), BF16),
+            pltpu.VMEM((slots, width), BF16),
+            pltpu.VMEM((slots, width), F32),
+            pltpu.VMEM((slots, heads), F32),
+            pltpu.VMEM((slots, heads), F32),
+            pltpu.VMEM((2 * half, tokens, rows), BF16),
+            pltpu.VMEM((2 * half, tokens, rows), BF16),
+            dma((depth, 2)), dma((depth,)),
+            dma((depth,)), dma((depth, 2)),
+            dma((depth,)), dma((depth,)),
+            dma((n,)), dma((n,)), dma((n,)), dma((n,)),
+            dma((n,)), dma((n,)), dma((n,)), dma((n,)),
+            dma((3,)), dma((3,)), dma((2,)), dma((2,)),
+            dma((2 * half,)), dma((2 * half,)),
+        ],
+        compiler_params=pltpu.CompilerParams(
+            collective_id=0, has_side_effects=True, vmem_limit_bytes=60 * 1024 * 1024
+        ),
+    )(x, dv, w, a, b, counts, storage)
+
+
 def solution(mesh):
     in_specs = (
         P(("group", "fsdp"), "tp"),
@@ -110,4 +467,7 @@
         P(("group", "fsdp"), None, "tp"),
         P(("group", "fsdp"), None, "tp"),
     )
-    return jax.shard_map(shards, mesh=mesh, in_specs=in_specs, out_specs=out_specs, check_vma=False)
+    shape = dict(mesh.shape)
+    paired = shape["group"] == 2 and shape["fsdp"] == 8 and shape["tp"] == 2
+    body = functools.partial(fused, shape["fsdp"]) if paired else shards
+    return jax.shard_map(body, mesh=mesh, in_specs=in_specs, out_specs=out_specs, check_vma=False)

time: 278 us -> 132 us (0.47)
  waiting for transfers between devices: 170 us -> 0 us
  Pallas kernels: 0 us -> 125 us
  blocking collectives: 35.6 us -> 0 us
  matrix products: 28.5 us -> 0 us
  other arithmetic: 13.2 us -> 0 us
  between operations: 13.8 us -> 0.66 us
  starting transfers between devices: 8.42 us -> 0 us
    all_gather x2 -> x0, waiting for transfers between devices: 125 us -> none  [the longest x1 125 us: shards(): lax.all_gather(fixed_projection_matrix, 'fsdp', axis=0, tiled=True)]
    pallas_call x0 -> x1, Pallas kernels: none -> 125 us  [fused(): pl.pallas_call(functools.partial(fused_kernel, fsdp_total), out_shape=(ja...]
    all_to_all x2 -> x0, waiting for transfers between devices: 43.3 us -> none  [the longest x1 42.6 us: shards(): lax.all_to_all(sent_down, 'fsdp', split_axis=0, concat_axis=1, tiled=True)]
    dot_general x8 -> x0, matrix products: 28.5 us -> none  [the longest x1 13.9 us: shards(): lax.dot_general(masked_rows, lax.all_gather(fixed_projection_matrix, 'fsd...]
    all_gather x1 -> x0, blocking collectives: 24.8 us -> none  [shards(): lax.all_gather(adapter_up_weight, 'fsdp', axis=0, tiled=True)]
    psum x1 -> x0, blocking collectives: 10.8 us -> none  [shards(): low_sum, middle_gradient_sum = lax.psum((low_part, inner_grad_piece), 'tp')]
    convert_element_type x1 -> x0, other arithmetic: 9.01 us -> none  [shards(): (frozen_output + adapter_contribution.reshape(token_rows, half_width)).as...]
    all_to_all x2 -> x0, starting transfers between devices: 8.3 us -> none  [the longest x1 4.88 us: shards(): lax.all_to_all(sent_down, 'fsdp', split_axis=0, concat_axis=1, tiled=True)]
  transfers between devices with their start and end apart: 5 -> 0, of which waited for: 3 -> 0; matrix products, arithmetic and copies ran while one was open for 14% -> 0% of each run, Pallas kernels for 0% -> 0%
where the time goes in v1:
time: 132 us
  Pallas kernels  125 us (95%)
  local copies, waits for them, and re-layouts  6.06 us (5%)
    pallas_call x1, Pallas kernels, fused(): pl.pallas_call(functools.partial(fused_kernel, fsdp_total), out_shape=(ja...  125 us
    unnamed x7, local copies, waits for them, and re-layouts  6.06 us

profile of v1, /device:TPU:1, one launch (start us, length us, event | category | flops | bytes accessed | tf_op | source)
XLA Modules:
  0.0 131.9 jit_solution(7731691953974714222)
XLA Ops:
  0.6 125.2 %shard_map.94 = (bf16[512,4096]{1,0:T(8,128)(2,1)}, f32[1,16,4096]{2,1,0:T(8,128)}, f32[1,16,512]{2,1,0:T(8,128)}) custom-call(bf16[512,4096]{1,0:T(8,128)(2,1)} %x_ref.1, bf16[512,512]{1,0:T(8,128)(2,1)} %dv_ref.1, bf16[1024,512]{1,0:T(8,128)(2,1)} %w_ref.1, bf16[1,16,4096]{2,1,0:T(8,128)(2,1)} %a_ref.1, bf16[1,16,512]{2,1,0:T(8,128)(2,1)} %b_ref.1, ...), custom_call_target="tpu_custom_call" | custom-call | tf_op jit(solution)/shard_map/pallas_call | solution.py:415
  125.9 0.0 copy-start
  125.9 0.0 copy-start.1
  125.9 4.7 %copy.13 = bf16[512,4096]{1,0:T(8,128)(2,1)} copy(bf16[512,4096]{1,0:T(8,128)(2,1)} %get-tuple-element.6) | data formatting | bytes 8388608
  130.6 0.0 copy-done
  130.6 0.7 copy.14
  131.3 0.0 copy-done.1
  131.3 0.6 copy.15
Async XLA Ops:
  125.9 4.8 %copy-start = (f32[1,16,4096]{2,1,0:T(8,128)S(1)}, f32[1,16,4096]{2,1,0:T(8,128)}, u32[]{:S(2)}) copy-start(f32[1,16,4096]{2,1,0:T(8,128)} %get-tuple-element.7) | copy-start | bytes 786436
  125.9 5.5 %copy-start.1 = (f32[1,16,512]{2,1,0:T(8,128)S(1)}, f32[1,16,512]{2,1,0:T(8,128)}, u32[]{:S(2)}) copy-start(f32[1,16,512]{2,1,0:T(8,128)} %get-tuple-element.8) | copy-start | bytes 98308

commit v2 on v1

--- a/solution.py
+++ b/solution.py
@@ -112,9 +112,9 @@
     x_ref, dv_ref, w_ref, a_ref, b_ref, cnt_ref, row_ref,
     ig_ref, lo_ref, ra_ref,
     wall, dvb, a_all, b_all, mask, gm, gm_t, psend, precv,
-    lsend, lrecv, lfull, rsend, rrecv, osend, orecv,
+    lsend, lcross, lrecv, lfull, rsend, rrecv, osend, orecv,
     ch_s, ch_r, y_s, y_r, sb_s, sb_r, a_s, a_r, b_s, b_r,
-    l_s, l_r, r_s, r_r, dv_s, dv_r, p_s, p_r, o_s, o_r,
+    l_s, lc_r, l_r, r_s, r_r, dv_s, dv_r, p_s, p_r, o_s, o_r,
 ):
     depth = fsdp_total // 2
     half = depth // 2
@@ -193,8 +193,17 @@
     def b_copy(j):
         return remote(b_all.at[mine, :], b_all.at[mine, :], b_s.at[j], b_r.at[f], (g, j, c))
 
-    def a_copy(j):
-        return remote(a_all.at[mine, :], a_all.at[mine, :], a_s.at[j], a_r.at[f], (g, j, c))
+    opposite = z * 2 + 1 - y
+
+    def a_copy(s, j):
+        part = a_all.at[rank_rows(s), :]
+        return remote(part, part, a_s.at[j * 2 + s % 2], a_r.at[s], (g, j, c))
+
+    def levels(fn):
+        def step(k, carry):
+            fn(lax.rem(z + k, depth))
+            return carry
+        lax.fori_loop(1, depth, step, 0)
 
     def peers(fn):
         def step(k, carry):
@@ -228,7 +237,8 @@
 
     dv_copy(1).start()
     spread(z)
-    peers(lambda j: a_copy(j).start())
+    a_copy(f, opposite).start()
+    levels(lambda zp: a_copy(f, zp * 2 + y).start())
 
     peers(lambda j: wait_in(b_all.at[rank_rows(j), :], b_r.at[j]))
     psend[0] = nt(dvb[0, c], b_all[...])
@@ -251,36 +261,39 @@
 
     lax.fori_loop(0, width // chunk, lower, 0)
 
-    def l_copy(j):
-        return remote(lsend.at[rank_rows(j), :], lrecv.at[mine, :], l_s.at[j], l_r.at[f], (g, j, c))
-
-    peers(lambda j: l_copy(j).start())
+    def l_cross(zp):
+        return remote(
+            lsend.at[rank_rows(zp * 2 + 1 - y), :], lcross.at[zp], l_s.at[zp * 2 + 1 - y], lc_r.at[zp], (g, opposite, c)
+        )
+
+    def l_copy(zp):
+        return remote(
+            lsend.at[rank_rows(zp * 2 + y), :], lrecv.at[z], l_s.at[zp * 2 + y], l_r.at[z], (g, zp * 2 + y, c)
+        )
+
+    levels(lambda zp: l_cross(zp).start())
+    l_cross(z).start()
+
+    wait_in(a_all.at[rank_rows(opposite), :], a_r.at[opposite])
+    levels(lambda zp: a_copy(opposite, zp * 2 + y).start())
 
     wait_in(dvb.at[1, c], dv_r.at[1])
     dv_copy(2).start()
 
-    peers(lambda j: wait_in(a_all.at[rank_rows(j), :], a_r.at[j]))
-    psend[1] = jnp.zeros((tokens, slots), F32)
-
-    def low_step(i, carry):
-        cols = pl.ds(pl.multiple_of(i * chunk, chunk), chunk)
-        psend[1] = psend[1] + nt(x_ref[:, cols], a_all[:, cols])
-        return carry
-
-    lax.fori_loop(0, width // chunk, low_step, 0)
-    low_copy = remote(psend.at[1], precv.at[1], p_s.at[1], p_r.at[1], sibling)
-    low_copy.start()
-    low_copy.wait_recv()
-    low = jnp.where(mask[...] > 0.5, psend[1] + precv[1], 0.0)
-    up_term = adapter_scale * jnp.dot(low.T.astype(BF16), dvb[0, c], preferred_element_type=F32)
-    rsend[...] = up_term
-
-    def r_copy(j):
-        return remote(rsend.at[rank_rows(j), :], rrecv.at[mine, :], r_s.at[j], r_r.at[f], (g, j, c))
-
-    peers(lambda j: r_copy(j).start())
     wait_in(dvb.at[0, 1 - c], dv_r.at[0])
     wait_in(dvb.at[1, 1 - c], dv_r.at[2])
+
+    def join(zp):
+        wait_in(lcross.at[zp], lc_r.at[zp])
+        place = rank_rows(zp * 2 + y)
+        lfull[place, :] = lfull[place, :] + lcross[zp].astype(F32)
+        lsend[place, :] = lfull[place, :].astype(BF16)
+        l_copy(zp).start()
+
+    def join_all():
+        levels(join)
+        wait_in(lcross.at[z], lc_r.at[z])
+        lfull[mine, :] = lfull[mine, :] + lcross[z].astype(F32)
 
     def o_copy(tile):
         return remote(osend.at[tile], orecv.at[tile], o_s.at[tile], o_r.at[tile], twin)
@@ -298,12 +311,6 @@
             tile = (zt - lo) * 2 + yp
             osend[tile] = (nt(dvb[1, 0], wall[zt, yp, 0]) + nt(dvb[1, 1], wall[zt, yp, 1])).astype(BF16)
             o_copy(tile).start()
-            cols = columns(tile, g)
-            ig_ref[:, cols] = (
-                nt(dvb[0, 0], wall[zt, yp, 0])
-                + nt(dvb[0, 1], wall[zt, yp, 1])
-                + jnp.dot(gm[...], a_all[:, cols], preferred_element_type=F32)
-            ).astype(BF16)
 
     def in_half(zp):
         return (zp >= lo) & (zp < lo + half)
@@ -337,7 +344,46 @@
 
         return carry
 
-    lax.fori_loop(1, depth + 1, step, 0)
+    lax.fori_loop(1, 2, step, 0)
+    join_all()
+    lax.fori_loop(2, depth, step, 0)
+
+    levels(lambda zp: wait_in(a_all.at[rank_rows(zp * 2 + y), :], a_r.at[zp * 2 + y]))
+    levels(lambda zp: wait_in(a_all.at[rank_rows(zp * 2 + 1 - y), :], a_r.at[zp * 2 + 1 - y]))
+    psend[1] = jnp.zeros((tokens, slots), F32)
+
+    def low_step(i, carry):
+        cols = pl.ds(pl.multiple_of(i * chunk, chunk), chunk)
+        psend[1] = psend[1] + nt(x_ref[:, cols], a_all[:, cols])
+        return carry
+
+    lax.fori_loop(0, width // chunk, low_step, 0)
+    low_copy = remote(psend.at[1], precv.at[1], p_s.at[1], p_r.at[1], sibling)
+    low_copy.start()
+    low_copy.wait_recv()
+    low = jnp.where(mask[...] > 0.5, psend[1] + precv[1], 0.0)
+    up_term = adapter_scale * jnp.dot(low.T.astype(BF16), dvb[0, c], preferred_element_type=F32)
+    rsend[...] = up_term
+
+    def r_copy(j):
+        return remote(rsend.at[rank_rows(j), :], rrecv.at[mine, :], r_s.at[j], r_r.at[f], (g, j, c))
+
+    peers(lambda j: r_copy(j).start())
+
+    lax.fori_loop(depth, depth + 1, step, 0)
+
+    def own_tile(tile, carry):
+        cols = columns(tile, g)
+        zt = lo + tile // 2
+        yp = tile % 2
+        ig_ref[:, cols] = (
+            nt(dvb[0, 0], wall[zt, yp, 0])
+            + nt(dvb[0, 1], wall[zt, yp, 1])
+            + jnp.dot(gm[...], a_all[:, cols], preferred_element_type=F32)
+        ).astype(BF16)
+        return carry
+
+    lax.fori_loop(0, 2 * half, own_tile, 0)
 
     def finish(tile, carry):
         wait_in(orecv.at[tile], o_r.at[tile])
@@ -354,12 +400,16 @@
     ra_ref[0] = rsend[mine, :]
 
     def add_terms(j):
-        wait_in(lrecv.at[rank_rows(j), :], l_r.at[j])
-        lo_ref[0] = lo_ref[0] + lrecv[rank_rows(j), :].astype(F32)
         wait_in(rrecv.at[rank_rows(j), :], r_r.at[j])
         ra_ref[0] = ra_ref[0] + rrecv[rank_rows(j), :]
 
     peers(add_terms)
+
+    def add_level(zp):
+        wait_in(lrecv.at[zp], l_r.at[zp])
+        lo_ref[0] = lo_ref[0] + lrecv[zp].astype(F32)
+
+    levels(add_level)
 
     for i in range(3):
         dv_copy(i).wait_send()
@@ -367,12 +417,20 @@
     low_copy.wait_send()
 
     def sent(j):
-        a_copy(j).wait_send()
         b_copy(j).wait_send()
-        l_copy(j).wait_send()
         r_copy(j).wait_send()
 
     peers(sent)
+    a_copy(f, opposite).wait_send()
+
+    def sent_level(zp):
+        a_copy(f, zp * 2 + y).wait_send()
+        a_copy(opposite, zp * 2 + y).wait_send()
+        l_cross(zp).wait_send()
+        l_copy(zp).wait_send()
+
+    levels(sent_level)
+    l_cross(z).wait_send()
 
     def sent_tile(tile, carry):
         o_copy(tile).wait_send()
@@ -432,7 +490,8 @@
             pltpu.VMEM((2, tokens, slots), F32),
             pltpu.VMEM((2, tokens, slots), F32),
             pltpu.VMEM((slots, width), BF16),
-            pltpu.VMEM((slots, width), BF16),
+            pltpu.VMEM((depth, rank, width), BF16),
+            pltpu.VMEM((depth, rank, width), BF16),
             pltpu.VMEM((slots, width), F32),
             pltpu.VMEM((slots, heads), F32),
             pltpu.VMEM((slots, heads), F32),
@@ -441,8 +500,8 @@
             dma((depth, 2)), dma((depth,)),
             dma((depth,)), dma((depth, 2)),
             dma((depth,)), dma((depth,)),
-            dma((n,)), dma((n,)), dma((n,)), dma((n,)),
-            dma((n,)), dma((n,)), dma((n,)), dma((n,)),
+            dma((2 * n,)), dma((n,)), dma((n,)), dma((n,)),
+            dma((n,)), dma((depth,)), dma((depth,)), dma((n,)), dma((n,)),
             dma((3,)), dma((3,)), dma((2,)), dma((2,)),
             dma((2 * half,)), dma((2 * half,)),
         ],

time: 132 us -> 113 us (0.86)
  Pallas kernels: 125 us -> 106 us
    pallas_call x1, Pallas kernels: 125 us -> 106 us  [fused(): pl.pallas_call(functools.partial(fused_kernel, fsdp_total), out_shape=(ja...]
where the time goes in v2:
time: 113 us; the launch traced here: 112 us
  Pallas kernels  106 us (94%)
  local copies, waits for them, and re-layouts  6.06 us (5%)
    pallas_call x1, Pallas kernels, fused(): pl.pallas_call(functools.partial(fused_kernel, fsdp_total), out_shape=(ja...  106 us
    unnamed x7, local copies, waits for them, and re-layouts  6.06 us

profile of v2, /device:TPU:1, one launch (start us, length us, event | category | flops | bytes accessed | tf_op | source)
XLA Modules:
  0.0 112.4 jit_solution(801587665745455619)
XLA Ops:
  0.6 105.7 %shard_map.94 = (bf16[512,4096]{1,0:T(8,128)(2,1)}, f32[1,16,4096]{2,1,0:T(8,128)}, f32[1,16,512]{2,1,0:T(8,128)}) custom-call(bf16[512,4096]{1,0:T(8,128)(2,1)} %x_ref.1, bf16[512,512]{1,0:T(8,128)(2,1)} %dv_ref.1, bf16[1024,512]{1,0:T(8,128)(2,1)} %w_ref.1, bf16[1,16,4096]{2,1,0:T(8,128)(2,1)} %a_ref.1, bf16[1,16,512]{2,1,0:T(8,128)(2,1)} %b_ref.1, ...), custom_call_target="tpu_custom_call" | custom-call | tf_op jit(solution)/shard_map/pallas_call | solution.py:473
  106.3 0.0 copy-start
  106.3 0.0 copy-start.1
  106.4 4.7 %copy.13 = bf16[512,4096]{1,0:T(8,128)(2,1)} copy(bf16[512,4096]{1,0:T(8,128)(2,1)} %get-tuple-element.6) | data formatting | bytes 8388608
  111.1 0.0 copy-done
  111.1 0.7 copy.14
  111.8 0.0 copy-done.1
  111.8 0.6 copy.15
Async XLA Ops:
  106.3 4.8 %copy-start = (f32[1,16,4096]{2,1,0:T(8,128)S(1)}, f32[1,16,4096]{2,1,0:T(8,128)}, u32[]{:S(2)}) copy-start(f32[1,16,4096]{2,1,0:T(8,128)} %get-tuple-element.7) | copy-start | bytes 786436
  106.3 5.5 %copy-start.1 = (f32[1,16,512]{2,1,0:T(8,128)S(1)}, f32[1,16,512]{2,1,0:T(8,128)}, u32[]{:S(2)}) copy-start(f32[1,16,512]{2,1,0:T(8,128)} %get-tuple-element.8) | copy-start | bytes 98308

commit v3 on v2

--- a/solution.py
+++ b/solution.py
@@ -101,6 +101,7 @@
 
 F32 = jnp.float32
 BF16 = jnp.bfloat16
+CUTS = 2
 
 
 def nt(a, b):
@@ -123,6 +124,7 @@
     rank = a_ref.shape[1]
     slots = fsdp_total * rank
     rows = w_ref.shape[0] // 2
+    part_rows = rows // CUTS
     g = lax.axis_index("group")
     f = lax.axis_index("fsdp")
     c = lax.axis_index("tp")
@@ -147,7 +149,9 @@
     for dev in (sibling, twin, (g, z * 2 + 1 - y, 1 - c)):
         pl.semaphore_signal(barrier, inc=1, device_id=dev, device_id_type=pl.DeviceIdType.MESH)
 
-    wall[z, y, c] = w_ref[pl.ds(pl.multiple_of(g * rows, rows), rows), :]
+    for h in range(CUTS):
+        at = pl.multiple_of(g * rows + h * part_rows, part_rows)
+        wall[z * CUTS + h, y, c] = w_ref[pl.ds(at, part_rows), :]
     mine = pl.ds(pl.multiple_of(f * rank, rank), rank)
     a_all[mine, :] = a_ref[0]
     b_all[mine, :] = b_ref[0]
@@ -176,19 +180,19 @@
             return remote(dvb.at[0, c], dvb.at[1, c], dv_s.at[1], dv_r.at[1], twin)
         return remote(dvb.at[1, c], dvb.at[1, c], dv_s.at[2], dv_r.at[2], sibling)
 
-    def piece(zp):
-        return wall.at[zp, y, c]
-
-    def chain_copy(zp, up):
+    def piece(q):
+        return wall.at[q, y, c]
+
+    def chain_copy(q, up):
         to = z + 1 if up else z - 1
-        return remote(piece(zp), piece(zp), ch_s.at[zp, 1 if up else 0], ch_r.at[zp], (g, to * 2 + y, c))
-
-    def y_copy(zp):
-        core = zp // half
-        return remote(piece(zp), piece(zp), y_s.at[zp], y_r.at[zp, c], (g, z * 2 + 1 - y, core))
-
-    def sib_copy(zp):
-        return remote(piece(zp), piece(zp), sb_s.at[zp], sb_r.at[zp], sibling)
+        return remote(piece(q), piece(q), ch_s.at[q, 1 if up else 0], ch_r.at[q], (g, to * 2 + y, c))
+
+    def y_copy(q):
+        core = q // (half * CUTS)
+        return remote(piece(q), piece(q), y_s.at[q], y_r.at[q, c], (g, z * 2 + 1 - y, core))
+
+    def sib_copy(q):
+        return remote(piece(q), piece(q), sb_s.at[q], sb_r.at[q], sibling)
 
     def b_copy(j):
         return remote(b_all.at[mine, :], b_all.at[mine, :], b_s.at[j], b_r.at[f], (g, j, c))
@@ -217,28 +221,29 @@
     def wait_in(dst, sem):
         remote(dst, dst, sem, sem, sibling).wait_recv()
 
-    def spread(zp):
-        y_copy(zp).start()
-
-        @pl.when(zp // half != c)
+    def spread(q):
+        y_copy(q).start()
+
+        @pl.when(q // (half * CUTS) != c)
         def _():
-            sib_copy(zp).start()
+            sib_copy(q).start()
 
     dv_copy(0).start()
     peers(lambda j: b_copy(j).start())
 
     @pl.when(z < depth - 1)
     def _():
-        chain_copy(z, True).start()
+        for h in range(CUTS):
+            chain_copy(z * CUTS + h, True).start()
 
     @pl.when(z > 0)
     def _():
-        chain_copy(z, False).start()
+        for h in range(CUTS):
+            chain_copy(z * CUTS + h, False).start()
 
     dv_copy(1).start()
-    spread(z)
-    a_copy(f, opposite).start()
-    levels(lambda zp: a_copy(f, zp * 2 + y).start())
+    for h in range(CUTS):
+        spread(z * CUTS + h)
 
     peers(lambda j: wait_in(b_all.at[rank_rows(j), :], b_r.at[j]))
     psend[0] = nt(dvb[0, c], b_all[...])
@@ -274,8 +279,6 @@
     levels(lambda zp: l_cross(zp).start())
     l_cross(z).start()
 
-    wait_in(a_all.at[rank_rows(opposite), :], a_r.at[opposite])
-    levels(lambda zp: a_copy(opposite, zp * 2 + y).start())
 
     wait_in(dvb.at[1, c], dv_r.at[1])
     dv_copy(2).start()
@@ -299,42 +302,49 @@
         return remote(osend.at[tile], orecv.at[tile], o_s.at[tile], o_r.at[tile], twin)
 
     def columns(tile, which):
-        return pl.ds(pl.multiple_of(tile * (2 * rows) + which * rows, rows), rows)
+        at = (tile // CUTS) * (2 * rows) + which * rows + (tile % CUTS) * part_rows
+        return pl.ds(pl.multiple_of(at, part_rows), part_rows)
 
     def tiles(zt):
-        wait_in(wall.at[zt, y, 1 - c], sb_r.at[zt])
-        for other in (0, 1):
-            yp = 1 - y if other else y
-            if other:
-                wait_in(wall.at[zt, yp, 0], y_r.at[zt, 0])
-                wait_in(wall.at[zt, yp, 1], y_r.at[zt, 1])
-            tile = (zt - lo) * 2 + yp
-            osend[tile] = (nt(dvb[1, 0], wall[zt, yp, 0]) + nt(dvb[1, 1], wall[zt, yp, 1])).astype(BF16)
-            o_copy(tile).start()
+        for h in range(CUTS):
+            q = zt * CUTS + h
+            wait_in(wall.at[q, y, 1 - c], sb_r.at[q])
+            for other in (0, 1):
+                yp = 1 - y if other else y
+                if other:
+                    wait_in(wall.at[q, yp, 0], y_r.at[q, 0])
+                    wait_in(wall.at[q, yp, 1], y_r.at[q, 1])
+                tile = ((zt - lo) * 2 + yp) * CUTS + h
+                osend[tile] = (nt(dvb[1, 0], wall[q, yp, 0]) + nt(dvb[1, 1], wall[q, yp, 1])).astype(BF16)
+                o_copy(tile).start()
 
     def in_half(zp):
         return (zp >= lo) & (zp < lo + half)
 
     def step(d, carry):
-        @pl.when(z - d >= 0)
-        def _():
-            wait_in(piece(z - d), ch_r.at[z - d])
-
-            @pl.when(z < depth - 1)
-            def _():
-                chain_copy(z - d, True).start()
-
-            spread(z - d)
-
-        @pl.when(z + d < depth)
-        def _():
-            wait_in(piece(z + d), ch_r.at[z + d])
-
-            @pl.when(z > 0)
-            def _():
-                chain_copy(z + d, False).start()
-
-            spread(z + d)
+        for h in range(CUTS):
+
+            @pl.when(z - d >= 0)
+            def _(h=h):
+                q = (z - d) * CUTS + h
+                wait_in(piece(q), ch_r.at[q])
+
+                @pl.when(z < depth - 1)
+                def _():
+                    chain_copy(q, True).start()
+
+                spread(q)
+
+            @pl.when(z + d < depth)
+            def _(h=h):
+                q = (z + d) * CUTS + h
+                wait_in(piece(q), ch_r.at[q])
+
+                @pl.when(z > 0)
+                def _():
+                    chain_copy(q, False).start()
+
+                spread(q)
 
         zt = jnp.where(in_half(z + d - 1), z + d - 1, z - d + 1)
 
@@ -346,7 +356,14 @@
 
     lax.fori_loop(1, 2, step, 0)
     join_all()
-    lax.fori_loop(2, depth, step, 0)
+    a_copy(f, opposite).start()
+    lax.fori_loop(2, 3, step, 0)
+    levels(lambda zp: a_copy(f, zp * 2 + y).start())
+    lax.fori_loop(3, depth, step, 0)
+
+    wait_in(a_all.at[rank_rows(opposite), :], a_r.at[opposite])
+    levels(lambda zp: a_copy(opposite, zp * 2 + y).start())
+    lax.fori_loop(depth, depth + 1, step, 0)
 
     levels(lambda zp: wait_in(a_all.at[rank_rows(zp * 2 + y), :], a_r.at[zp * 2 + y]))
     levels(lambda zp: wait_in(a_all.at[rank_rows(zp * 2 + 1 - y), :], a_r.at[zp * 2 + 1 - y]))
@@ -360,6 +377,19 @@
     lax.fori_loop(0, width // chunk, low_step, 0)
     low_copy = remote(psend.at[1], precv.at[1], p_s.at[1], p_r.at[1], sibling)
     low_copy.start()
+    def own_tile(tile, carry):
+        cols = columns(tile, g)
+        q = (lo + tile // (2 * CUTS)) * CUTS + tile % CUTS
+        yp = (tile // CUTS) % 2
+        ig_ref[:, cols] = (
+            nt(dvb[0, 0], wall[q, yp, 0])
+            + nt(dvb[0, 1], wall[q, yp, 1])
+            + jnp.dot(gm[...], a_all[:, cols], preferred_element_type=F32)
+        ).astype(BF16)
+        return carry
+
+    lax.fori_loop(0, 2 * half * CUTS, own_tile, 0)
+
     low_copy.wait_recv()
     low = jnp.where(mask[...] > 0.5, psend[1] + precv[1], 0.0)
     up_term = adapter_scale * jnp.dot(low.T.astype(BF16), dvb[0, c], preferred_element_type=F32)
@@ -369,21 +399,6 @@
         return remote(rsend.at[rank_rows(j), :], rrecv.at[mine, :], r_s.at[j], r_r.at[f], (g, j, c))
 
     peers(lambda j: r_copy(j).start())
-
-    lax.fori_loop(depth, depth + 1, step, 0)
-
-    def own_tile(tile, carry):
-        cols = columns(tile, g)
-        zt = lo + tile // 2
-        yp = tile % 2
-        ig_ref[:, cols] = (
-            nt(dvb[0, 0], wall[zt, yp, 0])
-            + nt(dvb[0, 1], wall[zt, yp, 1])
-            + jnp.dot(gm[...], a_all[:, cols], preferred_element_type=F32)
-        ).astype(BF16)
-        return carry
-
-    lax.fori_loop(0, 2 * half, own_tile, 0)
 
     def finish(tile, carry):
         wait_in(orecv.at[tile], o_r.at[tile])
@@ -394,7 +409,7 @@
         ).astype(BF16)
         return carry
 
-    lax.fori_loop(0, 2 * half, finish, 0)
+    lax.fori_loop(0, 2 * half * CUTS, finish, 0)
 
     lo_ref[0] = lfull[mine, :]
     ra_ref[0] = rsend[mine, :]
@@ -436,26 +451,26 @@
         o_copy(tile).wait_send()
         return carry
 
-    lax.fori_loop(0, 2 * half, sent_tile, 0)
-
-    def sent_piece(zp, carry):
-        @pl.when((zp <= z) & (z < depth - 1))
+    lax.fori_loop(0, 2 * half * CUTS, sent_tile, 0)
+
+    def sent_piece(q, carry):
+        @pl.when((q // CUTS <= z) & (z < depth - 1))
         def _():
-            chain_copy(zp, True).wait_send()
-
-        @pl.when((zp >= z) & (z > 0))
+            chain_copy(q, True).wait_send()
+
+        @pl.when((q // CUTS >= z) & (z > 0))
         def _():
-            chain_copy(zp, False).wait_send()
-
-        y_copy(zp).wait_send()
-
-        @pl.when(zp // half != c)
+            chain_copy(q, False).wait_send()
+
+        y_copy(q).wait_send()
+
+        @pl.when(q // (half * CUTS) != c)
         def _():
-            sib_copy(zp).wait_send()
-
-        return carry
-
-    lax.fori_loop(0, depth, sent_piece, 0)
+            sib_copy(q).wait_send()
+
+        return carry
+
+    lax.fori_loop(0, depth * CUTS, sent_piece, 0)
 
 
 def fused(fsdp_total, x, dv, w, a, b, counts, storage):
@@ -480,7 +495,7 @@
         in_specs=[vmem] * 5 + [smem] * 2,
         out_specs=(vmem,) * 3,
         scratch_shapes=[
-            pltpu.VMEM((depth, 2, 2, rows, heads), BF16),
+            pltpu.VMEM((depth * CUTS, 2, 2, rows // CUTS, heads), BF16),
             pltpu.VMEM((2, 2, tokens, heads), BF16),
             pltpu.VMEM((slots, width), BF16),
             pltpu.VMEM((slots, heads), BF16),
@@ -495,15 +510,15 @@
             pltpu.VMEM((slots, width), F32),
             pltpu.VMEM((slots, heads), F32),
             pltpu.VMEM((slots, heads), F32),
-            pltpu.VMEM((2 * half, tokens, rows), BF16),
-            pltpu.VMEM((2 * half, tokens, rows), BF16),
-            dma((depth, 2)), dma((depth,)),
-            dma((depth,)), dma((depth, 2)),
-            dma((depth,)), dma((depth,)),
+            pltpu.VMEM((2 * half * CUTS, tokens, rows // CUTS), BF16),
+            pltpu.VMEM((2 * half * CUTS, tokens, rows // CUTS), BF16),
+            dma((depth * CUTS, 2)), dma((depth * CUTS,)),
+            dma((depth * CUTS,)), dma((depth * CUTS, 2)),
+            dma((depth * CUTS,)), dma((depth * CUTS,)),
             dma((2 * n,)), dma((n,)), dma((n,)), dma((n,)),
             dma((n,)), dma((depth,)), dma((depth,)), dma((n,)), dma((n,)),
             dma((3,)), dma((3,)), dma((2,)), dma((2,)),
-            dma((2 * half,)), dma((2 * half,)),
+            dma((2 * half * CUTS,)), dma((2 * half * CUTS,)),
         ],
         compiler_params=pltpu.CompilerParams(
             collective_id=0, has_side_effects=True, vmem_limit_bytes=60 * 1024 * 1024

time: 113 us -> 98 us (0.87)
  Pallas kernels: 106 us -> 89.9 us
    pallas_call x1, Pallas kernels: 106 us -> 89.9 us  [fused(): pl.pallas_call(functools.partial(fused_kernel, fsdp_total), out_shape=(ja...]
where the time goes in v3:
time: 98 us; the launch traced here: 96.6 us
  Pallas kernels  89.9 us (92%)
  local copies, waits for them, and re-layouts  6.06 us (6%)
    pallas_call x1, Pallas kernels, fused(): pl.pallas_call(functools.partial(fused_kernel, fsdp_total), out_shape=(ja...  89.9 us
    unnamed x7, local copies, waits for them, and re-layouts  6.06 us

profile of v3, /device:TPU:1, one launch (start us, length us, event | category | flops | bytes accessed | tf_op | source)
XLA Modules:
  0.0 96.6 jit_solution(6007001626198063547)
XLA Ops:
  0.6 89.9 %shard_map.94 = (bf16[512,4096]{1,0:T(8,128)(2,1)}, f32[1,16,4096]{2,1,0:T(8,128)}, f32[1,16,512]{2,1,0:T(8,128)}) custom-call(bf16[512,4096]{1,0:T(8,128)(2,1)} %x_ref.1, bf16[512,512]{1,0:T(8,128)(2,1)} %dv_ref.1, bf16[1024,512]{1,0:T(8,128)(2,1)} %w_ref.1, bf16[1,16,4096]{2,1,0:T(8,128)(2,1)} %a_ref.1, bf16[1,16,512]{2,1,0:T(8,128)(2,1)} %b_ref.1, ...), custom_call_target="tpu_custom_call" | custom-call | tf_op jit(solution)/shard_map/pallas_call | solution.py:488
  90.5 0.0 copy-start
  90.5 0.0 copy-start.1
  90.5 4.7 %copy.13 = bf16[512,4096]{1,0:T(8,128)(2,1)} copy(bf16[512,4096]{1,0:T(8,128)(2,1)} %get-tuple-element.6) | data formatting | bytes 8388608
  95.3 0.0 copy-done
  95.3 0.7 copy.14
  96.0 0.0 copy-done.1
  96.0 0.6 copy.15
Async XLA Ops:
  90.5 4.8 %copy-start = (f32[1,16,4096]{2,1,0:T(8,128)S(1)}, f32[1,16,4096]{2,1,0:T(8,128)}, u32[]{:S(2)}) copy-start(f32[1,16,4096]{2,1,0:T(8,128)} %get-tuple-element.7) | copy-start | bytes 786436
  90.5 5.5 %copy-start.1 = (f32[1,16,512]{2,1,0:T(8,128)S(1)}, f32[1,16,512]{2,1,0:T(8,128)}, u32[]{:S(2)}) copy-start(f32[1,16,512]{2,1,0:T(8,128)} %get-tuple-element.8) | copy-start | bytes 98308
